TPU v7x, 128 devices: a whole 4x4x4 slice. The times are simulated.
128 devices in a mesh: blocks: 32 (over z, y, core), loads: 4 (over x).
Axes of the slice: x: 4, y: 4, z: 4, core: 2. Of those that a mesh axis runs over, the one named last changes fastest.
Arguments:
- design: float32 [256, 96, 128], P('blocks'), may hold values from 0.05 to 1
- free_mask: int32 [256, 96, 128], P('blocks'), may hold values 0 or 1
- heat_load: float32 [4, 256, 96, 128], P('loads', 'blocks'), may hold values from -6 to 6
Outputs:
- temperature: float32 [4, 256, 96, 128], P('loads', 'blocks')
- smoothed_objective_slope: float32 [256, 96, 128], P('blocks')
Inputs may be any that keep to these rules, and one draw needn't show every extreme that they name: `free_mask`: 1 marks a free cell, 0 a cell held at zero temperature.
All inputs are finite; a program needn't handle non-finite values. No bound on the sum of `free_mask` on one device may be relied on, other than what follows from the above.
Results may differ from a plain program's by a relative error of at most 0.0001.
Values sent between devices are 32-bit elements; how exact they have to be, the bound alone decides.
A program may use at most 128 MiB of HBM per device.

v0:
```python
import math

import jax
import jax.numpy as jnp
from jax import lax
from jax.sharding import PartitionSpec as P

ITERS = 2
SWEEPS = 2
LEVELS = 4


COND_FLOOR = 0.01
PENALTY = 3.0
RELAX_FACTOR = 2.0 / 3.0
HELD_DIAGONAL = 6.0
WEIGHT_CENTER = 1.5
WEIGHT_FACE = 0.5
WEIGHT_EDGE = 1.5 - math.sqrt(2.0)


def extended(value, sides, width):
    for axis, dim in sides:
        peers, length = (lax.axis_size(axis), value.shape[dim])
        up = [(i, (i + 1) % peers) for i in range(peers - 1)]
        down = [(j, i) for i, j in up]
        last = lax.slice_in_dim(value, length - width, length, axis=dim)
        initial = lax.slice_in_dim(value, 0, width, axis=dim)
        before = lax.ppermute(last, axis, up)
        after = lax.ppermute(initial, axis, down)
        value = jnp.concatenate([before, value, after], axis=dim)
    return value


def pad_sides(values):
    return jnp.pad(values, ((0, 0), (1, 1), (1, 1)))


def grid_rim(values):
    return extended(values, (("blocks", 0),), 1)


def conduct_rim(values):
    return extended(values, (("blocks", 0),), 1)


def inner_total(first_vec, second_vec):
    return lax.psum(jnp.sum(first_vec * second_vec), "blocks")


def blur_padded(bordered_array):
    extent = (bordered_array.shape[0] - 2, bordered_array.shape[1] - 2, bordered_array.shape[2] - 2)

    def shifted(translate_first_axis, shift_y, displaced_depth):
        return bordered_array[
            1 + translate_first_axis : 1 + translate_first_axis + extent[0],
            1 + shift_y : 1 + shift_y + extent[1],
            1 + displaced_depth : 1 + displaced_depth + extent[2],
        ]

    face_part = jnp.zeros(extent, jnp.float32)
    edge_part = jnp.zeros(extent, jnp.float32)
    for translate_first_axis in (-1, 0, 1):
        for shift_y in (-1, 0, 1):
            for displaced_depth in (-1, 0, 1):
                reach = abs(translate_first_axis) + abs(shift_y) + abs(displaced_depth)
                if reach == 1:
                    face_part = face_part + shifted(translate_first_axis, shift_y, displaced_depth)
                elif reach == 2:
                    edge_part = edge_part + shifted(translate_first_axis, shift_y, displaced_depth)
    return WEIGHT_CENTER * shifted(0, 0, 0) + WEIGHT_FACE * face_part + WEIGHT_EDGE * edge_part


def face_set(padded_ends, spacing):
    center_cells = padded_ends[1:-1]
    sided = pad_sides(center_cells)
    minus_x = spacing * 0.5 * (center_cells + padded_ends[:-2])
    plus_x = spacing * 0.5 * (center_cells + padded_ends[2:])
    minus_y = spacing * 0.5 * (center_cells + sided[:, :-2, 1:-1])
    plus_y = spacing * 0.5 * (center_cells + sided[:, 2:, 1:-1])
    minus_z = spacing * 0.5 * (center_cells + sided[:, 1:-1, :-2])
    plus_z = spacing * 0.5 * (center_cells + sided[:, 1:-1, 2:])
    plain_diagonal = minus_x + plus_x + minus_y + plus_y + minus_z + plus_z
    return ((minus_x, plus_x, minus_y, plus_y, minus_z, plus_z), plain_diagonal)


def apply_padded(padded_ends, coeffs, plain_diagonal):
    center_cells = padded_ends[1:-1]
    sided = pad_sides(center_cells)
    beside = coeffs[0] * padded_ends[:-2] + coeffs[1] * padded_ends[2:]
    beside = beside + coeffs[2] * sided[:, :-2, 1:-1] + coeffs[3] * sided[:, 2:, 1:-1]
    beside = beside + coeffs[4] * sided[:, 1:-1, :-2] + coeffs[5] * sided[:, 1:-1, 2:]
    return plain_diagonal * center_cells - beside


def face_energy(padded_ends):
    center_cells = padded_ends[1:-1]
    sided = pad_sides(center_cells)
    summed = (center_cells - padded_ends[:-2]) ** 2 + (center_cells - padded_ends[2:]) ** 2
    summed = (
        summed
        + (center_cells - sided[:, :-2, 1:-1]) ** 2
        + (center_cells - sided[:, 2:, 1:-1]) ** 2
    )
    summed = (
        summed
        + (center_cells - sided[:, 1:-1, :-2]) ** 2
        + (center_cells - sided[:, 1:-1, 2:]) ** 2
    )
    return 0.5 * summed


def restrict_sum(values):
    shape_x, shape_y, shape_z = values.shape
    return values.reshape(shape_x // 2, 2, shape_y // 2, 2, shape_z // 2, 2).sum(axis=(1, 3, 5))


def prolong(values):
    shape_x, shape_y, shape_z = values.shape
    spread = jnp.broadcast_to(
        values[:, None, :, None, :, None], (shape_x, 2, shape_y, 2, shape_z, 2)
    )
    return spread.reshape(2 * shape_x, 2 * shape_y, 2 * shape_z)


def level_apply(values, hierarchy_entries):
    coeffs, plain_diagonal, jacobi, free_share = hierarchy_entries
    if free_share is None:
        return apply_padded(grid_rim(values), coeffs, plain_diagonal)
    masked = free_share * values
    inner_part = apply_padded(grid_rim(masked), coeffs, plain_diagonal)
    return free_share * inner_part + (1.0 - free_share) * HELD_DIAGONAL * values


def smooth_cycle(right_side, start, grades):
    hierarchy_entries = grades[start]
    jacobi = hierarchy_entries[2]
    iterate = RELAX_FACTOR * right_side / jacobi
    iterate = (
        iterate + RELAX_FACTOR * (right_side - level_apply(iterate, hierarchy_entries)) / jacobi
    )
    if start + 1 < len(grades):
        equation_mismatch = right_side - level_apply(iterate, hierarchy_entries)
        correction = smooth_cycle(0.5 * restrict_sum(equation_mismatch), start + 1, grades)
        iterate = iterate + prolong(correction)
    for sweep_count in range(SWEEPS):
        iterate = (
            iterate + RELAX_FACTOR * (right_side - level_apply(iterate, hierarchy_entries)) / jacobi
        )
    return iterate


def solve_case(scenario_heating, free_share, grades):
    right_side = free_share * scenario_heating
    answer_vector = jnp.zeros_like(right_side)
    mismatch_vector = right_side
    precond = smooth_cycle(mismatch_vector, 0, grades)
    direction = precond
    inner_now = inner_total(mismatch_vector, precond)
    for iteration in range(ITERS):
        product_image = level_apply(direction, grades[0])
        step_length = inner_now / inner_total(direction, product_image)
        answer_vector = answer_vector + step_length * direction
        mismatch_vector = mismatch_vector - step_length * product_image
        if iteration + 1 < ITERS:
            precond = smooth_cycle(mismatch_vector, 0, grades)
            inner_next = inner_total(mismatch_vector, precond)
            direction = precond + inner_next / inner_now * direction
            inner_now = inner_next
    return answer_vector


def body(design, free_mask, heat_load):
    slab_rows = design.shape[0]
    position = lax.axis_index("blocks")
    members = lax.axis_size("blocks")
    row_ids = jnp.arange(slab_rows + 2)
    inside = (row_ids >= 1) & (row_ids <= slab_rows)
    inside = (
        inside
        | (row_ids == 0) & (position > 0)
        | (row_ids == slab_rows + 1) & (position < members - 1)
    )
    ones_padded = jnp.broadcast_to(
        inside.astype(jnp.float32)[:, None, None], (slab_rows + 2, design.shape[1], design.shape[2])
    )
    weight_total = blur_padded(pad_sides(ones_padded))
    design_padded = extended(design, (("blocks", 0),), 1)
    density = blur_padded(pad_sides(design_padded)) / weight_total
    conduct = COND_FLOOR + (1.0 - COND_FLOOR) * density**PENALTY
    free_share = free_mask.astype(jnp.float32)
    grades = []
    current = conduct
    spacing = 1.0
    for number in range(LEVELS):
        coeffs, plain_diagonal = face_set(conduct_rim(current), spacing)
        if number == 0:
            grades.append(
                (
                    coeffs,
                    plain_diagonal,
                    free_share * plain_diagonal + (1.0 - free_share) * HELD_DIAGONAL,
                    free_share,
                )
            )
        else:
            grades.append((coeffs, plain_diagonal, plain_diagonal, None))
        if number + 1 < LEVELS:
            current = 0.125 * restrict_sum(current)
            spacing = 2.0 * spacing
    answer_vector = solve_case(heat_load[0], free_share, grades)
    masked_temp = extended(free_share * answer_vector, (("blocks", 0),), 1)
    element_energy = face_energy(masked_temp)
    energy = lax.psum(element_energy, "loads")
    gradient = -PENALTY * (1.0 - COND_FLOOR) * density ** (PENALTY - 1.0) * energy
    bordered_array = extended(gradient / weight_total, (("blocks", 0),), 1)
    smoothed_objective_slope = blur_padded(pad_sides(bordered_array))
    return (answer_vector[None], smoothed_objective_slope)


def solution(mesh):
    return jax.shard_map(
        body,
        mesh=mesh,
        in_specs=(
            P("blocks", None, None),
            P("blocks", None, None),
            P("loads", "blocks", None, None),
        ),
        out_specs=(P("loads", "blocks", None, None), P("blocks", None, None)),
        check_vma=False,
    )
```

profile of v0, /device:TPU:1, one launch (start us, length us, event | category | flops | bytes accessed | tf_op | source)
XLA Modules:
  0.0 867.6 jit_solution(15342600082157584584)
XLA Ops:
  28.3 26.5 %reshape.159 = f32[4,2,48,2,64,2]{5,4,3,2,1,0:T(8,128)} reshape(f32[8,96,128]{2,1,0:T(8,128)S(1)} %get-tuple-element.49) | data formatting | bytes 786432 | tf_op jit(solution)/shard_map/reshape | solution.py:115
  54.8 9.5 %reduce_sum.139 = f32[4,48,64]{2,1,0:T(8,128)S(1)} reduce(f32[4,2,48,2,64,2]{5,4,3,2,1,0:T(8,128)} %reshape.159, f32[]{:T(128)} %constant.23.clone.1), dimensions={1,3,5}, to_apply=%region_1.2 | reduce | flops 86016 | bytes 442372 | tf_op jit(solution)/shard_map/reduce_sum | solution.py:115
  94.9 27.3 %reshape.158 = f32[4,2,48,2,64,2]{5,4,3,2,1,0:T(8,128)} reshape(f32[8,96,128]{2,1,0:T(8,128)} %fusion.38) | data formatting | bytes 786432 | tf_op jit(solution)/shard_map/reshape | solution.py:115
  122.2 9.4 %reduce_sum.138 = f32[4,48,64]{2,1,0:T(8,128)S(1)} reduce(f32[4,2,48,2,64,2]{5,4,3,2,1,0:T(8,128)} %reshape.158, f32[]{:T(128)} %constant.23.clone.1), dimensions={1,3,5}, to_apply=%region_0.1 | reduce | flops 86016 | bytes 442372 | tf_op jit(solution)/shard_map/reduce_sum | solution.py:115
  158.2 5.1 reshape.160
  187.8 7.3 collective-permute-start.20
  227.2 6.5 collective-permute-start.28
  245.6 5.7 collective-permute-done.31
  266.6 7.2 collective-permute-done.33
  280.0 7.5 collective-permute-done.35
  287.7 9.2 %broadcast_in_dim.72 = f32[4,2,48,2,64,2]{5,4,3,2,1,0:T(8,128)} broadcast(f32[4,48,64]{2,1,0:T(8,128)S(1)} %fusion.288), dimensions={0,2,4} | broadcast | bytes 442368 | tf_op jit(solution)/shard_map/broadcast_in_dim | solution.py:120
  297.0 18.8 %reshape.162 = f32[8,96,128]{2,1,0:T(8,128)} reshape(f32[4,2,48,2,64,2]{5,4,3,2,1,0:T(8,128)} %broadcast_in_dim.72) | data formatting | bytes 786432 | tf_op jit(solution)/shard_map/reshape | solution.py:123
  321.3 5.1 collective-permute-done.37
  331.4 5.1 collective-permute-done.39
  341.5 5.1 collective-permute-done.41
  348.7 58.8 %all-reduce.40 = (f32[]{:T(128)}, f32[]{:T(128)}) all-reduce(f32[]{:T(128)} %get-tuple-element.3, f32[]{:T(128)} %get-tuple-element.2), channel_id=1, replica_groups=mesh['blocks'=32,'loads'=4] {'blocks'}, use_global_device_ids=true, to_apply=%region_9.10 | all-reduce | flops 2 | bytes 16 | tf_op jit(solution)/shard_map/psum | solution.py:48
  413.1 5.2 collective-permute-start.43
  428.6 27.3 %reshape.163 = f32[4,2,48,2,64,2]{5,4,3,2,1,0:T(8,128)} reshape(f32[8,96,128]{2,1,0:T(8,128)} %fusion.106) | data formatting | bytes 786432 | tf_op jit(solution)/shard_map/reshape | solution.py:115
  455.9 10.1 %reduce_sum.150 = f32[4,48,64]{2,1,0:T(8,128)} reduce(f32[4,2,48,2,64,2]{5,4,3,2,1,0:T(8,128)} %reshape.163, f32[]{:T(128)} %constant.23.clone.1), dimensions={1,3,5}, to_apply=%region_12.13 | reduce | flops 86016 | bytes 442372 | tf_op jit(solution)/shard_map/reduce_sum | solution.py:115
  479.7 8.1 collective-permute-done.49
  488.5 5.1 reshape.164
  562.5 5.1 collective-permute-done.63
  583.0 7.2 collective-permute-done.65
  597.6 7.6 collective-permute-done.67
  605.4 9.2 %broadcast_in_dim.78 = f32[4,2,48,2,64,2]{5,4,3,2,1,0:T(8,128)} broadcast(f32[4,48,64]{2,1,0:T(8,128)S(1)} %fusion.337), dimensions={0,2,4} | broadcast | bytes 442368 | tf_op jit(solution)/shard_map/broadcast_in_dim | solution.py:120
  614.6 18.8 %reshape.166 = f32[8,96,128]{2,1,0:T(8,128)} reshape(f32[4,2,48,2,64,2]{5,4,3,2,1,0:T(8,128)} %broadcast_in_dim.78) | data formatting | bytes 786432 | tf_op jit(solution)/shard_map/reshape | solution.py:123
  648.7 5.1 collective-permute-done.71
  655.9 58.8 %psum.37 = f32[]{:T(128)} all-reduce(f32[]{:T(128)} %get-tuple-element.6), channel_id=1, replica_groups=mesh['blocks'=32,'loads'=4] {'blocks'}, use_global_device_ids=true, to_apply=%region_17.18 | all-reduce | flops 1 | bytes 8 | tf_op jit(solution)/shard_map/psum | solution.py:48
  720.1 5.2 collective-permute-start.73
  727.4 63.0 %psum.38 = f32[]{:T(128)} all-reduce(f32[]{:T(128)} %fusion.237), channel_id=1, replica_groups=mesh['blocks'=32,'loads'=4] {'blocks'}, use_global_device_ids=true, to_apply=%region_19.20 | all-reduce | flops 1 | bytes 8 | tf_op jit(solution)/shard_map/psum | solution.py:48
  801.1 43.7 %all-reduce.43.cloned.1.call-done = f32[8,96,128]{2,1,0:T(8,128)} async-done(((f32[8,96,128]{2,1,0:T(8,128)}), f32[8,96,128]{2,1,0:T(8,128)}) %all-reduce.43.cloned.1.call-update) | async-done | bytes 393232 | tf_op jit(solution)/shard_map/psum | solution.py:214
  847.0 5.8 collective-permute-start.76
  (351 shorter events, 348.2 us)
Async XLA Ops:
  7.2 837.7 %all-reduce.43.cloned.1.call-start = ((), (), s32[]{:S(2)}) async-start(), calls=%async_computation | async-start | bytes 786432 | tf_op jit(solution)/shard_map/psum | solution.py:214
  22.7 41.6 %collective-permute-start.3 = (f32[1,96,128]{2,1,0:T(8,128)S(1)}, f32[1,96,128]{2,1,0:T(8,128)S(1)}, u32[]{:S(2)}, u32[]{:S(2)}) collective-permute-start(f32[1,96,128]{2,1,0:T(8,128)S(1)} %get-tuple-element.77), channel_id=1, source_target_pairs={{4,0},{8,4},{12,8},{16,12},{20,16},{24,20},{28,24},{32,28},{36,32}... | collective-permute-start | bytes 147464 | tf_op jit(solution)/shard_map/ppermute | solution.py:30
  24.6 39.7 %collective-permute-start.2 = (f32[1,96,128]{2,1,0:T(8,128)S(1)}, f32[1,96,128]{2,1,0:T(8,128)S(1)}, u32[]{:S(2)}, u32[]{:S(2)}) collective-permute-start(f32[1,96,128]{2,1,0:T(8,128)S(1)} %get-tuple-element.78), channel_id=1, source_target_pairs={{0,4},{4,8},{8,12},{12,16},{16,20},{20,24},{24,28},{28,32},{32,36}... | collective-permute-start | bytes 147464 | tf_op jit(solution)/shard_map/ppermute | solution.py:29
  73.6 17.7 %collective-permute-start.6 = (f32[1,96,128]{2,1,0:T(8,128)S(1)}, f32[1,96,128]{2,1,0:T(8,128)S(1)}, u32[]{:S(2)}, u32[]{:S(2)}) collective-permute-start(f32[1,96,128]{2,1,0:T(8,128)S(1)} %get-tuple-element.73), channel_id=1, source_target_pairs={{0,4},{4,8},{8,12},{12,16},{16,20},{20,24},{24,28},{28,32},{32,36}... | collective-permute-start | bytes 147464 | tf_op jit(solution)/shard_map/ppermute | solution.py:29
  75.5 15.8 %collective-permute-start.7 = (f32[1,96,128]{2,1,0:T(8,128)S(1)}, f32[1,96,128]{2,1,0:T(8,128)S(1)}, u32[]{:S(2)}, u32[]{:S(2)}) collective-permute-start(f32[1,96,128]{2,1,0:T(8,128)S(1)} %get-tuple-element.74), channel_id=1, source_target_pairs={{4,0},{8,4},{12,8},{16,12},{20,16},{24,20},{28,24},{32,28},{36,32}... | collective-permute-start | bytes 147464 | tf_op jit(solution)/shard_map/ppermute | solution.py:30
  83.4 48.2 %collective-permute-start.8 = (f32[1,48,64]{2,1,0:T(8,128)}, f32[1,48,64]{2,1,0:T(8,128)S(1)}, u32[]{:S(2)}, u32[]{:S(2)}) collective-permute-start(f32[1,48,64]{2,1,0:T(8,128)} %get-tuple-element.97), channel_id=1, source_target_pairs={{0,4},{4,8},{8,12},{12,16},{16,20},{20,24},{24,28},{28,32},{32,36}... | collective-permute-start | bytes 36872 | tf_op jit(solution)/shard_map/ppermute | solution.py:29
  86.6 45.6 %collective-permute-start.9 = (f32[1,48,64]{2,1,0:T(8,128)}, f32[1,48,64]{2,1,0:T(8,128)}, u32[]{:S(2)}, u32[]{:S(2)}) collective-permute-start(f32[1,48,64]{2,1,0:T(8,128)} %get-tuple-element.98), channel_id=1, source_target_pairs={{4,0},{8,4},{12,8},{16,12},{20,16},{24,20},{28,24},{32,28},{36,32}... | collective-permute-start | bytes 36872 | tf_op jit(solution)/shard_map/ppermute | solution.py:30
  137.4 7.2 collective-permute-start.11
  144.7 12.6 %collective-permute-start.12 = (f32[1,48,64]{2,1,0:T(8,128)S(1)}, f32[1,48,64]{2,1,0:T(8,128)S(1)}, u32[]{:S(2)}, u32[]{:S(2)}) collective-permute-start(f32[1,48,64]{2,1,0:T(8,128)S(1)} %get-tuple-element.93), channel_id=1, source_target_pairs={{0,4},{4,8},{8,12},{12,16},{16,20},{20,24},{24,28},{28,32},{32,36}... | collective-permute-start | bytes 36872 | tf_op jit(solution)/shard_map/ppermute | solution.py:29
  147.6 9.8 %collective-permute-start.13 = (f32[1,48,64]{2,1,0:T(8,128)S(1)}, f32[1,48,64]{2,1,0:T(8,128)S(1)}, u32[]{:S(2)}, u32[]{:S(2)}) collective-permute-start(f32[1,48,64]{2,1,0:T(8,128)S(1)} %get-tuple-element.94), channel_id=1, source_target_pairs={{4,0},{8,4},{12,8},{16,12},{20,16},{24,20},{28,24},{32,28},{36,32}... | collective-permute-start | bytes 36872 | tf_op jit(solution)/shard_map/ppermute | solution.py:30
  150.1 15.9 %collective-permute-start.14 = (f32[1,24,32]{2,1,0:T(8,128)}, f32[1,24,32]{2,1,0:T(8,128)}, u32[]{:S(2)}, u32[]{:S(2)}) collective-permute-start(f32[1,24,32]{2,1,0:T(8,128)} %get-tuple-element.117), channel_id=1, source_target_pairs={{0,4},{4,8},{8,12},{12,16},{16,20},{20,24},{24,28},{28,32},{32,36}... | collective-permute-start | bytes 9224 | tf_op jit(solution)/shard_map/ppermute | solution.py:29
  155.0 11.1 %collective-permute-start.15 = (f32[1,24,32]{2,1,0:T(8,128)}, f32[1,24,32]{2,1,0:T(8,128)}, u32[]{:S(2)}, u32[]{:S(2)}) collective-permute-start(f32[1,24,32]{2,1,0:T(8,128)} %get-tuple-element.118), channel_id=1, source_target_pairs={{4,0},{8,4},{12,8},{16,12},{20,16},{24,20},{28,24},{32,28},{36,32}... | collective-permute-start | bytes 9224 | tf_op jit(solution)/shard_map/ppermute | solution.py:30
  169.1 7.4 collective-permute-start.16
  179.6 15.4 %collective-permute-start.18 = (f32[1,24,32]{2,1,0:T(8,128)S(1)}, f32[1,24,32]{2,1,0:T(8,128)S(1)}, u32[]{:S(2)}, u32[]{:S(2)}) collective-permute-start(f32[1,24,32]{2,1,0:T(8,128)S(1)} %get-tuple-element.113), channel_id=1, source_target_pairs={{0,4},{4,8},{8,12},{12,16},{16,20},{20,24},{24,28},{28,32},{32,36}... | collective-permute-start | bytes 9224 | tf_op jit(solution)/shard_map/ppermute | solution.py:29
  183.9 11.2 %collective-permute-start.19 = (f32[1,24,32]{2,1,0:T(8,128)S(1)}, f32[1,24,32]{2,1,0:T(8,128)S(1)}, u32[]{:S(2)}, u32[]{:S(2)}) collective-permute-start(f32[1,24,32]{2,1,0:T(8,128)S(1)} %get-tuple-element.114), channel_id=1, source_target_pairs={{4,0},{8,4},{12,8},{16,12},{20,16},{24,20},{28,24},{32,28},{36,32}... | collective-permute-start | bytes 9224 | tf_op jit(solution)/shard_map/ppermute | solution.py:30
  185.8 13.9 %collective-permute-start.21 = (f32[1,12,16]{2,1,0:T(8,128)S(1)}, f32[1,12,16]{2,1,0:T(8,128)}, u32[]{:S(2)}, u32[]{:S(2)}) collective-permute-start(f32[1,12,16]{2,1,0:T(8,128)S(1)} %multiply_bitcast_fusion), channel_id=1, source_target_pairs={{4,0},{8,4},{12,8},{16,12},{20,16},{24,20},{28,24},{32,28},{36,32}... | collective-permute-start | bytes 2312 | tf_op jit(solution)/shard_map/ppermute | solution.py:30
  187.8 12.0 %collective-permute-start.20 = (f32[1,12,16]{2,1,0:T(8,128)S(1)}, f32[1,12,16]{2,1,0:T(8,128)}, u32[]{:S(2)}, u32[]{:S(2)}) collective-permute-start(f32[1,12,16]{2,1,0:T(8,128)S(1)} %multiply_bitcast_fusion), channel_id=1, source_target_pairs={{0,4},{4,8},{8,12},{12,16},{16,20},{20,24},{24,28},{28,32},{32,36}... | collective-permute-start | bytes 2312 | tf_op jit(solution)/shard_map/ppermute | solution.py:29
  227.2 8.4 collective-permute-start.28
  243.6 7.6 collective-permute-start.31
  264.7 9.2 %collective-permute-start.33 = (f32[1,48,64]{2,1,0:T(8,128)S(1)}, f32[1,48,64]{2,1,0:T(8,128)S(1)}, u32[]{:S(2)}, u32[]{:S(2)}) collective-permute-start(f32[1,48,64]{2,1,0:T(8,128)S(1)} %get-tuple-element.92), channel_id=1, source_target_pairs={{4,0},{8,4},{12,8},{16,12},{20,16},{24,20},{28,24},{32,28},{36,32}... | collective-permute-start | bytes 36872 | tf_op jit(solution)/shard_map/ppermute | solution.py:30
  278.1 9.5 %collective-permute-start.35 = (f32[1,48,64]{2,1,0:T(8,128)S(1)}, f32[1,48,64]{2,1,0:T(8,128)S(1)}, u32[]{:S(2)}, u32[]{:S(2)}) collective-permute-start(f32[1,48,64]{2,1,0:T(8,128)S(1)} %get-tuple-element.90), channel_id=1, source_target_pairs={{4,0},{8,4},{12,8},{16,12},{20,16},{24,20},{28,24},{32,28},{36,32}... | collective-permute-start | bytes 36872 | tf_op jit(solution)/shard_map/ppermute | solution.py:30
  318.9 7.5 collective-permute-start.37
  329.0 7.5 collective-permute-start.39
  339.1 7.5 collective-permute-start.41
  409.9 8.4 collective-permute-start.42
  477.6 10.2 %collective-permute-start.49 = (f32[1,48,64]{2,1,0:T(8,128)S(1)}, f32[1,48,64]{2,1,0:T(8,128)S(1)}, u32[]{:S(2)}, u32[]{:S(2)}) collective-permute-start(f32[1,48,64]{2,1,0:T(8,128)S(1)} %get-tuple-element.86), channel_id=1, source_target_pairs={{4,0},{8,4},{12,8},{16,12},{20,16},{24,20},{28,24},{32,28},{36,32}... | collective-permute-start | bytes 36872 | tf_op jit(solution)/shard_map/ppermute | solution.py:30
  581.0 9.2 %collective-permute-start.65 = (f32[1,48,64]{2,1,0:T(8,128)S(1)}, f32[1,48,64]{2,1,0:T(8,128)S(1)}, u32[]{:S(2)}, u32[]{:S(2)}) collective-permute-start(f32[1,48,64]{2,1,0:T(8,128)S(1)} %get-tuple-element.84), channel_id=1, source_target_pairs={{4,0},{8,4},{12,8},{16,12},{20,16},{24,20},{28,24},{32,28},{36,32}... | collective-permute-start | bytes 36872 | tf_op jit(solution)/shard_map/ppermute | solution.py:30
  595.4 9.8 %collective-permute-start.67 = (f32[1,48,64]{2,1,0:T(8,128)S(1)}, f32[1,48,64]{2,1,0:T(8,128)S(1)}, u32[]{:S(2)}, u32[]{:S(2)}) collective-permute-start(f32[1,48,64]{2,1,0:T(8,128)S(1)} %get-tuple-element.82), channel_id=1, source_target_pairs={{4,0},{8,4},{12,8},{16,12},{20,16},{24,20},{28,24},{32,28},{36,32}... | collective-permute-start | bytes 36872 | tf_op jit(solution)/shard_map/ppermute | solution.py:30
  636.5 7.2 collective-permute-start.69
  646.3 7.5 collective-permute-start.71
  717.0 8.3 collective-permute-start.72
  847.0 7.7 collective-permute-start.76
  (96 other events, 2153.2 us)
Sparse Core Ops, SparseCore 0:
  801.3 43.5 all-reduce.42
where the time goes:
time: 882 us; the launch traced here: 868 us
  starting transfers between devices  224 us (25%)
  blocking collectives  181 us (21%)
  local copies, waits for them, and re-layouts  179 us (20%)
  waiting for transfers between devices  165 us (19%)
  other arithmetic  99.9 us (11%)
  between operations  19.8 us (2%)
    psum x3, blocking collectives, inner_total(): return lax.psum(jnp.sum(first_vec * second_vec), 'blocks')  181 us
    ppermute x39, starting transfers between devices, extended(): before = lax.ppermute(last, axis, up)  136 us
    ppermute x39, waiting for transfers between devices, extended(): after = lax.ppermute(initial, axis, down)  116 us
    reshape x5, local copies, waits for them, and re-layouts, restrict_sum(): values.reshape(shape_x // 2, 2, shape_y // 2, 2, shape_z // 2, 2)  91.3 us
    ppermute x39, starting transfers between devices, extended(): after = lax.ppermute(initial, axis, down)  88.1 us
    reshape x4, local copies, waits for them, and re-layouts, prolong(): return spread.reshape(2 * shape_x, 2 * shape_y, 2 * shape_z)  46.6 us
    reduce_sum x12, other arithmetic, restrict_sum(): values.reshape(shape_x // 2, 2, shape_y // 2, 2, shape_z // 2, 2)  45.5 us
    psum x1, waiting for transfers between devices, body(): energy = lax.psum(element_energy, 'loads')  43.7 us
  transfers between devices with their start and end apart: 79, of which 33 were waited for; matrix products, arithmetic and copies ran while one was open for 12% of the time, Pallas kernels for 0%

commit v1 on v0

v1 whole, which is shorter than its diff:
```python
import math

import jax
import jax.numpy as jnp
from jax import lax
from jax.experimental import pallas as pl
from jax.experimental.pallas import tpu as pltpu
from jax.sharding import PartitionSpec as P

F32 = jnp.float32
BF16 = jnp.bfloat16
MESH = pl.DeviceIdType.MESH
EDGE = 1.5 - math.sqrt(2.0)
THIRD = 1.0 / 3.0
RELAX = 2.0 / 3.0
NB = 32
NLOAD = 4
ROWS = 96
OWN = 8
REACH = 6
WIN = 2 * REACH + 1


def up_y(v):
    return pltpu.roll(v, v.shape[0] - 1, 0)


def dn_y(v):
    return pltpu.roll(v, 1, 0)


def up_z(v):
    return pltpu.roll(v, 127, 1)


def dn_z(v):
    return pltpu.roll(v, 1, 1)


def lanes(shape):
    return lax.broadcasted_iota(jnp.int32, shape, len(shape) - 1)


def rows_of(shape):
    return lax.broadcasted_iota(jnp.int32, shape, len(shape) - 2)


def exact_dot(x, m):
    hi = x.astype(BF16)
    rest = x - hi.astype(F32)
    mid = rest.astype(BF16)
    low = (rest - mid.astype(F32)).astype(BF16)
    d = lambda a: jnp.dot(a, m, preferred_element_type=F32)
    return d(hi) + d(mid) + d(low)


def stencil(x, xm, xp, cxm, cx, cy, cz):
    s = cx * xp + cxm * xm
    s = s + (cy * up_y(x) + dn_y(cy * x))
    return s + (cz * up_z(x) + dn_z(cz * x))


def loop(a, b, fn, u=0):
    n = b - a
    u = u or next(k for k in (4, 3, 2) if n % k == 0)
    assert n % u == 0

    def step(i, c):
        for k in range(u):
            fn(a + i * u + k)
        return c

    lax.fori_loop(0, n // u, step, 0)


def fold(v):
    return v.reshape(v.shape[0] // 8, 8, 128).sum(axis=0)


def z_sum(f):
    lane = lanes(f.shape)
    return jnp.where(lane == 0, 0.0, dn_z(f)) + jnp.where(lane == 127, 0.0, up_z(f))


def y_sum(f):
    row = rows_of(f.shape)
    last = f.shape[0] - 1
    return jnp.where(row == 0, 0.0, dn_y(f)) + jnp.where(row == last, 0.0, up_y(f))


def blur(f, s):
    h = 0.5 * f + EDGE * s
    zf = z_sum(f)
    return 1.5 * f + 0.5 * s + z_sum(h) + y_sum(h + EDGE * zf)


def kernel(design, mask, heat, temp_out, slope_out, D, MK, HT, COND, CX, CY, CZ, G, J, X, Y, B0, Z0, Q0,
           VA, VB, EA, EB, EC, W0, W1, DW, T0, PT0, C1, CX1, CY1, CZ1, G1, J1, X1, Y1, B1, T1, PT1, CP, CR, BP, BR,
           MP, MR, C2, MC, R, MG, CXU2, CXD2, CY2, CZ2, G2, J2, X2, T3, CX3, CY3, CZ3, G3, J3, PT2,
           AR, EN, RS, GB, TOZ1, TOZ2A, TOZ2B, TOZ3, FRZ1, FRZ2A, FRZ2B, FRZ3, lsem, ssem, rsem):
    me = lax.axis_index("blocks")
    mx = lax.axis_index("loads")

    def block(o):
        return {"blocks": lax.rem(me + o + NB, NB)}

    def load(o):
        return {"loads": lax.rem(mx + o, NLOAD)}

    local = [
        pltpu.make_async_copy(design, D.at[pl.ds(8, 8)], lsem.at[0]),
        pltpu.make_async_copy(mask, MK.at[pl.ds(8, 8)], lsem.at[1]),
        pltpu.make_async_copy(heat.at[0], HT.at[pl.ds(8, 8)], lsem.at[2]),
    ]
    for c in local:
        c.start()

    barrier = pltpu.get_barrier_semaphore()

    def greet(o, c):
        pl.semaphore_signal(barrier, inc=1, device_id=block(o), device_id_type=MESH)
        return c

    lax.fori_loop(1, NB, greet, 0)
    for o in range(1, NLOAD):
        for device in (load(o), {**block(1), **load(o)}, {**block(-1), **load(o)}):
            pl.semaphore_signal(barrier, inc=1, device_id=device, device_id_type=MESH)

    def joined(l, first=7, last=15):
        ends = ((me == 0) & (l == first)) | ((me == NB - 1) & (l == last))
        return jnp.where(ends, 0.0, 1.0).astype(F32)

    def density(l):
        md, mu = joined(l - 1), joined(l)
        weight = W0[...] + (md + mu) * W1[...]
        return blur(D[l], md * D[l - 1] + mu * D[l + 1]) / weight, weight

    def conduct(l):
        d, _ = density(l)
        COND[l] = 0.01 + 0.99 * (d * d * d)

    for c in local:
        c.wait()
    pl.semaphore_wait(barrier, NB - 1 + 3 * (NLOAD - 1))

    sent = []
    count = [0]

    def together(copies, size):
        k = count[0]
        count[0] += 1
        for src, dst, device in copies:
            pltpu.make_async_remote_copy(
                src_ref=src, dst_ref=dst, send_sem=ssem.at[k], recv_sem=rsem.at[k], device_id=device, device_id_type=MESH
            ).start()
        c = pltpu.make_async_remote_copy(
            src_ref=size, dst_ref=size, send_sem=ssem.at[k], recv_sem=rsem.at[k], device_id=block(1), device_id_type=MESH
        )
        sent.append(c)
        return c

    def rim(ref, a, b):
        n = b - a
        return [
            (ref.at[pl.ds(a + 8, n)], ref.at[pl.ds(a, n)], block(1)),
            (ref.at[pl.ds(16 - b, n)], ref.at[pl.ds(24 - b, n)], block(-1)),
        ]

    def layers(n):
        return D.at[pl.ds(0, n)]

    def gather(msg, buf):
        buf[REACH] = msg[...]
        offsets = [s for o in range(1, REACH + 1) for s in (o, -o)]
        return together([(msg, buf.at[REACH - s], block(s)) for s in offsets], buf.at[pl.ds(0, WIN - 1)])

    def reduce_start(values, buf):
        k = count[0]
        count[0] += 1
        lane = lanes((1, 128))
        row = jnp.zeros((1, 128), F32)
        for i, v in enumerate(values):
            row = jnp.where(lane == i, jnp.sum(v), row)
        buf[me] = row

        def send(i, c):
            o = i
            pltpu.make_async_remote_copy(
                src_ref=buf.at[me], dst_ref=buf.at[me], send_sem=ssem.at[k], recv_sem=rsem.at[k],
                device_id=block(o), device_id_type=MESH,
            ).start()
            return c

        lax.fori_loop(1, NB, send, 0)
        c = pltpu.make_async_remote_copy(
            src_ref=buf.at[pl.ds(0, NB - 1)], dst_ref=buf.at[pl.ds(0, NB - 1)], send_sem=ssem.at[k],
            recv_sem=rsem.at[k], device_id=block(1), device_id_type=MESH,
        )
        sent.append(c)
        return c

    def reduce_done(c, buf, n):
        c.wait_recv()
        total = jnp.sum(buf[...], axis=0)
        return [total[:, i : i + 1] for i in range(n)]

    e_design = together(rim(D, 4, 8), layers(8))
    e_mask = together(rim(MK, 5, 8), layers(6))
    e_heat = together(rim(HT, 6, 8), layers(4))

    ii = lax.broadcasted_iota(jnp.int32, (128, 128), 0)
    jj = lax.broadcasted_iota(jnp.int32, (128, 128), 1)
    half_i = lax.shift_right_logical(ii, 1)
    half_j = lax.shift_right_logical(jj, 1)
    put = lambda ref, cond: ref.__setitem__(Ellipsis, jnp.where(cond, 1.0, 0.0).astype(BF16))
    put(TOZ1, half_i == jj)
    put(TOZ2A, (half_i == jj) & (ii < 64))
    put(TOZ2B, (half_i + 32 == jj) & (ii < 64))
    put(TOZ3, (lax.shift_right_logical(ii & 31, 1) == jj) & (ii < 64))
    put(FRZ1, half_j == ii)
    put(FRZ2A, (half_j == ii) & (jj < 64))
    put(FRZ2B, (half_j + 32 == ii) & (jj < 64))
    put(FRZ3, (lax.shift_right_logical(jj & 31, 1) == ii) & (jj < 64))
    plane = (ROWS, 128)
    lane0, row0 = lanes(plane), rows_of(plane)
    one = lambda cond: jnp.where(cond, 1.0, 0.0)
    nz = 2.0 - one(lane0 == 0) - one(lane0 == 127)
    ny = 2.0 - one(row0 == 0) - one(row0 == ROWS - 1)
    W0[...] = 1.5 + 0.5 * (ny + nz) + EDGE * (ny * nz)
    W1[...] = 0.5 + EDGE * (ny + nz)
    T3[pl.ds(312, 8), :] = jnp.zeros((8, 128), F32)
    COND[0] = jnp.zeros(plane, F32)


    def free(l):
        return MK[l].astype(F32)

    def faces(l):
        c = COND[l]
        md, mu = joined(l - 1), joined(l)
        f = free(l)
        cp = COND[l + 1]
        last_row, last_lane = rows_of(plane) == ROWS - 1, lanes(plane) == 127
        first_row, first_lane = rows_of(plane) == 0, lanes(plane) == 0
        cyp = jnp.where(last_row, 0.0, up_y(c))
        czp = jnp.where(last_lane, 0.0, up_z(c))
        cym = jnp.where(first_row, 0.0, dn_y(c))
        czm = jnp.where(first_lane, 0.0, dn_z(c))
        CX[l] = (0.5 * mu) * (c + cp) * (f * free(l + 1))
        CY[l] = jnp.where(last_row, 0.0, 0.5 * (c + cyp) * (f * up_y(f)))
        CZ[l] = jnp.where(last_lane, 0.0, 0.5 * (c + czp) * (f * up_z(f)))
        diag = 3.0 * c + 0.5 * (mu * cp + md * COND[l - 1] + (cyp + cym) + (czp + czm))
        j = f * diag + (1.0 - f) * 6.0
        J[l] = j
        G[l] = RELAX / j

    def right_side(l):
        b = free(l) * HT[l]
        B0[l] = b
        X[l] = G[l] * b

    loop(9, 15, conduct)
    loop(10, 14, faces)
    loop(10, 14, right_side)
    e_design.wait_recv()
    loop(5, 9, conduct)
    loop(15, 19, conduct)

    def pair_z1(n, scale):
        rows = T0[pl.ds(0, n * 48, 2), :] + T0[pl.ds(1, n * 48, 2), :]
        return (exact_dot(rows, TOZ1[...]) * scale).reshape(n, 48, 128)

    def pair_cond(i):
        T0[pl.ds(pl.multiple_of(i * 96, 8), 96), :] = COND[8 + 2 * i] + COND[9 + 2 * i]

    loop(0, 4, pair_cond)
    C1[pl.ds(4, 4)] = pair_z1(4, 0.125)
    CP[0] = C1[4] + pltpu.roll(C1[5], 64, 1)
    CP[1] = C1[6] + pltpu.roll(C1[7], 64, 1)
    e_cond = together([(CP, CR.at[0], block(1)), (CP, CR.at[1], block(-1))], CR)

    def pair_z2(src, msg, scale):
        for i in range(2):
            T1[pl.ds(48 * i, 48), :] = src(2 * i) + src(2 * i + 1)
        rows = T1[pl.ds(0, 48, 2), :] + T1[pl.ds(1, 48, 2), :]
        msg[...] = (exact_dot(rows[:24], TOZ2A[...]) + exact_dot(rows[24:], TOZ2B[...])) * scale


    e_mask.wait_recv()
    loop(6, 10, faces)
    loop(14, 18, faces)
    e_heat.wait_recv()
    loop(6, 10, right_side)
    loop(14, 18, right_side)

    def apply0(ref, l):
        return stencil(ref[l], ref[l - 1], ref[l + 1], CX[l - 1], CX[l], CY[l], CZ[l])

    def sweep0(src, dst, b):
        def one_layer(l):
            dst[l] = src[l] * THIRD + G[l] * (b[l] + apply0(src, l))

        return one_layer

    def residual0(src, b, first):
        def pair(i):
            total = None
            for k in range(2):
                l = first + 2 * i + k
                r = b[l] - J[l] * src[l] + apply0(src, l)
                total = r if total is None else total + r
            T0[pl.ds(pl.multiple_of(i * 96, 8), 96), :] = total

        return pair

    def apply1(ref, l):
        return stencil(ref[l], ref[l - 1], ref[l + 1], CX1[l - 1], CX1[l], CY1[l], CZ1[l])

    def sweep1(src, dst):
        def one_layer(l):
            dst[l] = src[l] * THIRD + G1[l] * (B1[l] + apply1(src, l))

        return one_layer

    def faces1():
        shape = (48, 128)
        lane, row = lanes(shape), rows_of(shape)
        for side, base in ((0, 0), (1, 8)):
            for i in range(2):
                v = CR[side, i]
                C1[base + 2 * i] = jnp.where(lane < 64, v, 0.0)
                C1[base + 2 * i + 1] = jnp.where(lane < 64, pltpu.roll(v, 64, 1), 0.0)
        CX1[0] = C1[0] + C1[1]

        def one_layer(l):
            c = C1[l]
            md, mu = joined(l - 1, 3, 7), joined(l, 3, 7)
            cp = C1[l + 1]
            cyp = jnp.where(row == 47, 0.0, up_y(c))
            czp = up_z(c)
            cym = jnp.where(row == 0, 0.0, dn_y(c))
            czm = dn_z(c)
            CX1[l] = mu * (c + cp)
            CY1[l] = jnp.where(row == 47, 0.0, c + cyp)
            CZ1[l] = jnp.where(lane >= 63, 0.0, c + czp)
            diag = 6.0 * c + (mu * cp + md * C1[l - 1] + (cyp + cym) + (czp + czm))
            j = jnp.where(lane < 64, diag, 1.0)
            J1[l] = j
            G1[l] = RELAX / j

        loop(1, 11, one_layer)

    def level1_down(msg, packed):
        def start(l):
            X1[l] = G1[l] * B1[l]

        loop(2, 10, start, 4)
        loop(3, 9, sweep1(X1, Y1))
        for l in range(4):
            packed[l] = Y1[4 + l] + pltpu.roll(B1[4 + l], 64, 1)

        def mismatch(i):
            l = 4 + i
            return B1[l] - J1[l] * Y1[l] + apply1(Y1, l)

        pair_z2(mismatch, msg, 0.5)

    def level1_up(recv, a):
        for side, base in ((0, 0), (1, 8)):
            for i in range(4):
                v = recv[side, i]
                Y1[base + i] = v
                B1[base + i] = pltpu.roll(v, 64, 1)
        for l in range(a, 12 - a):
            X1[l] = Y1[l] + PT1[(l % 4) // 2, pl.ds(48 * (l // 4), 48), :]
        loop(a + 1, 11 - a, sweep1(X1, Y1))
        loop(a + 2, 10 - a, sweep1(Y1, X1))

    wide = (WIN * 24, 128)
    lane2 = lanes(wide)
    block2 = lax.broadcasted_iota(jnp.int32, (WIN, 24, 128), 0).reshape(wide)
    y2 = lax.broadcasted_iota(jnp.int32, (WIN, 24, 128), 1).reshape(wide)
    cut = lax.rem(NB - 1 - me + REACH, NB)

    def around2(v):
        n = v.shape[0]
        lane = lanes(v.shape)
        plus, minus = pltpu.roll(v, 32, 1), pltpu.roll(v, 96, 1)
        above = jnp.where(lane < 32, minus, pltpu.roll(plus, n - 24, 0))
        below = jnp.where(lane < 32, pltpu.roll(minus, 24, 0), plus)
        return above, below

    def faces2():
        c = C2[...].reshape(wide)
        above, below = around2(c)
        low = lane2 < 32
        used = lane2 < 64
        above = jnp.where((block2 == cut) & (lane2 >= 32), 0.0, above)
        below = jnp.where((block2 == cut + 1) & low, 0.0, below)
        cyp = jnp.where(y2 == 23, 0.0, up_y(c))
        cym = jnp.where(y2 == 0, 0.0, dn_y(c))
        zl = lane2 & 31
        czp = jnp.where(zl == 31, 0.0, up_z(c))
        czm = jnp.where(zl == 0, 0.0, dn_z(c))
        cut_up = ((block2 == cut) & (lane2 >= 32)) | (lane2 >= 64)
        cut_down = ((block2 == cut + 1) & low) | (lane2 >= 64)
        CXU2[...] = jnp.where(cut_up, 0.0, 2.0 * (c + above))
        CXD2[...] = jnp.where(cut_down, 0.0, 2.0 * (c + below))
        CY2[...] = jnp.where(y2 == 23, 0.0, 2.0 * (c + cyp))
        CZ2[...] = jnp.where((zl == 31) | (lane2 >= 64), 0.0, 2.0 * (c + czp))
        diag = 12.0 * c + 2.0 * ((above + below) + (cyp + cym) + (czp + czm))
        j = jnp.where(used, diag, 1.0)
        J2[...] = j
        G2[...] = RELAX / j
        T3[pl.ds(0, 312), :] = exact_dot(c, TOZ3[...])
        c3 = (T3[pl.ds(0, 160, 2), :] + T3[pl.ds(1, 160, 2), :]) * 0.125
        shape = (160, 128)
        lane, row = lanes(shape), rows_of(shape)
        blk = lax.shift_right_logical(row * 5462, 16)
        y = row - 12 * blk
        a3 = jnp.where(blk == cut, 0.0, pltpu.roll(c3, 148, 0))
        b3 = jnp.where(blk == cut + 1, 0.0, pltpu.roll(c3, 12, 0))
        yp = jnp.where(y == 11, 0.0, up_y(c3))
        ym = jnp.where(y == 0, 0.0, dn_y(c3))
        zp, zm = up_z(c3), dn_z(c3)
        CX3[...] = jnp.where(blk == cut, 0.0, 4.0 * (c3 + a3))
        CY3[...] = jnp.where(y == 11, 0.0, 4.0 * (c3 + yp))
        CZ3[...] = jnp.where(lane >= 15, 0.0, 4.0 * (c3 + zp))
        diag3 = 24.0 * c3 + 4.0 * ((a3 + b3) + (yp + ym) + (zp + zm))
        j3 = jnp.where((lane < 16) & (row < 156), diag3, 1.0)
        J3[...] = j3
        G3[...] = RELAX / j3

    def apply2(x, part):
        above, below = around2(x)
        cy, cz = CY2[part, :], CZ2[part, :]
        s = CXU2[part, :] * above + CXD2[part, :] * below
        s = s + (cy * up_y(x) + dn_y(cy * x))
        return s + (cz * up_z(x) + dn_z(cz * x))

    def apply3(x):
        cx, cy, cz = CX3[...], CY3[...], CZ3[...]
        s = cx * pltpu.roll(x, 148, 0) + pltpu.roll(cx * x, 12, 0)
        s = s + (cy * up_y(x) + dn_y(cy * x))
        return s + (cz * up_z(x) + dn_z(cz * x))

    def coarse(buf):
        whole = pl.ds(0, WIN * 24)
        b = buf[...].reshape(wide)
        x = G2[...] * b
        x = x * THIRD + G2[...] * (b + apply2(x, whole))
        X2[...] = x
        r = b - J2[...] * x + apply2(x, whole)
        T3[pl.ds(0, 312), :] = exact_dot(r, TOZ3[...])
        b3 = (T3[pl.ds(0, 160, 2), :] + T3[pl.ds(1, 160, 2), :]) * 0.5
        g3 = G3[...]
        x3 = g3 * b3
        for _ in range(3):
            x3 = x3 * THIRD + g3 * (b3 + apply3(x3))
        spread = exact_dot(x3[48:112], FRZ3[...])
        PT2[pl.ds(0, 64, 2), :] = spread
        PT2[pl.ds(1, 64, 2), :] = spread
        part = pl.ds(96, 120)
        b = buf[pl.ds(4, 5)].reshape(120, 128)
        x = X2[part, :] + PT2[pl.ds(0, 120), :]
        g = G2[part, :]
        for _ in range(2):
            x = x * THIRD + g * (b + apply2(x, part))
        x = x[24:96]
        for k, m in enumerate((FRZ2A, FRZ2B)):
            spread = exact_dot(x, m[...])
            PT1[k, pl.ds(0, 72, 2), :] = spread
            PT1[k, pl.ds(1, 72, 2), :] = spread

    def spread0(first, n):
        x = X1[pl.ds(first, n)].reshape(n * 48, 128)
        spread = exact_dot(x, FRZ1[...])
        PT0[pl.ds(0, n * 48, 2), :] = spread
        PT0[pl.ds(1, n * 48, 2), :] = spread

        def add(i):
            p = PT0[pl.ds(pl.multiple_of(i * 96, 8), 96), :]
            l = 2 * (first + i)
            X[l] = Y[l] + p
            X[l + 1] = Y[l + 1] + p

        loop(0, n, add)

    loop(7, 17, sweep0(X, Y, B0))
    loop(0, 4, residual0(Y, B0, 8), 1)
    B1[pl.ds(4, 4)] = pair_z1(4, 0.5)
    BP[0] = B1[4] + pltpu.roll(B1[5], 64, 1)
    BP[1] = B1[6] + pltpu.roll(B1[7], 64, 1)
    e_b1 = together([(BP.at[1], BR.at[0], block(1)), (BP.at[0], BR.at[1], block(-1))], BR)
    pair_z2(lambda i: C1[4 + i], MC, 0.125)
    g_cond = gather(MC, C2)
    e_next = together(rim(D, 3, 4) + rim(MK, 4, 5) + rim(HT, 5, 6), layers(6))
    e_cond.wait_recv()
    faces1()
    e_b1.wait_recv()
    for side, base in ((0, 2), (1, 8)):
        B1[base] = BR[side]
        B1[base + 1] = pltpu.roll(BR[side], 64, 1)
    level1_down(MG.at[0], MP.at[0])
    g_one = gather(MG.at[0], R.at[0])
    e_m1 = together([(MP.at[0], MR.at[0, 0], block(1)), (MP.at[0], MR.at[0, 1], block(-1))], MR.at[0])

    e_rest = together(rim(D, 0, 3) + rim(MK, 1, 4), layers(12))

    g_cond.wait_recv()
    faces2()

    def slope_factor(l):
        d, weight = density(l)
        DW[l - 8] = (-3.0 * 0.99) * (d * d) / weight

    loop(8, 16, slope_factor)
    e_next.wait_recv()
    for l in (4, 19):
        conduct(l)
    for l in (5, 18):
        faces(l)
    for l in (5, 18):
        right_side(l)
    for l in (6, 17):
        sweep0(X, Y, B0)(l)

    g_one.wait_recv()
    coarse(R.at[0])
    e_m1.wait_recv()
    level1_up(MR.at[0], 1)
    spread0(3, 6)
    loop(7, 17, sweep0(X, Y, B0))
    post = sweep0(Y, Z0, B0)
    loop(8, 16, post)
    e_near = together(rim(Z0, 4, 8), layers(8))
    e_far = together(rim(Z0, 1, 4), layers(6))

    def image(l):
        q = J[l] * Z0[l] - apply0(Z0, l)
        Q0[l] = q
        X[l] = G[l] * q

    loop(9, 15, image)
    e_rest.wait_recv()
    loop(1, 4, conduct, 1)
    loop(20, 23, conduct, 1)
    loop(1, 5, faces)
    loop(19, 22, faces, 1)
    e_near.wait_recv()
    loop(5, 9, image)
    loop(15, 19, image)

    def inner0(i, c):
        l = OWN + i
        z = Z0[l]
        return c[0] + fold(B0[l] * z), c[1] + fold(z * Q0[l])

    nil = jnp.zeros((8, 128), F32)
    ar0 = reduce_start(lax.fori_loop(0, 8, inner0, (nil, nil)), AR.at[0])
    pre = sweep0(X, Y, Q0)
    mismatch0 = residual0(Y, Q0, 4)
    loop(6, 18, pre)
    loop(2, 6, mismatch0, 1)
    e_far.wait_recv()
    loop(2, 5, image, 1)
    loop(19, 22, image, 1)
    loop(3, 6, pre, 1)
    loop(18, 21, pre, 1)
    loop(0, 2, mismatch0, 1)
    loop(6, 8, mismatch0, 1)
    B1[pl.ds(2, 8)] = pair_z1(8, 0.5)
    level1_down(MG.at[1], MP.at[1])
    g_two = gather(MG.at[1], R.at[1])
    e_m2 = together([(MP.at[1], MR.at[1, 0], block(1)), (MP.at[1], MR.at[1, 1], block(-1))], MR.at[1])

    def masked(l):
        VA[l] = free(l) * Z0[l]

    loop(7, 17, masked)
    rho0, pq0 = reduce_done(ar0, AR.at[0], 2)
    a0 = rho0 / pq0
    g_two.wait_recv()
    coarse(R.at[1])
    e_m2.wait_recv()
    level1_up(MR.at[1], 0)
    spread0(2, 8)
    loop(6, 18, sweep0(X, Y, Q0))

    def last_sweep(l):
        w = Y[l] * THIRD + G[l] * (Q0[l] + apply0(Y, l))
        z = Z0[l] - a0 * w
        X[l] = z
        VB[l] = free(l) * z

    loop(7, 17, last_sweep)

    def inner1(i, c):
        l = OWN + i
        z = X[l]
        bz = J[l] * z - apply0(X, l)
        q = Q0[l]
        r = B0[l] - a0 * q
        return c[0] + fold(r * z), c[1] + fold(z * bz), c[2] + fold(z * q)

    ar1 = reduce_start(lax.fori_loop(0, 8, inner1, (nil, nil, nil)), AR.at[1])

    def forms(l):
        md, mu = joined(l - 1), joined(l)
        row, lane = rows_of(plane), lanes(plane)
        a, b = VA[l], VB[l]

        def gaps(ref, v):
            return (
                v - md * ref[l - 1],
                v - mu * ref[l + 1],
                v - jnp.where(row == ROWS - 1, 0.0, up_y(v)),
                v - jnp.where(lane == 127, 0.0, up_z(v)),
            )

        ga, gb = gaps(VA, a), gaps(VB, b)

        def form(g, h, vv):
            dy, dz = g[2] * h[2], g[3] * h[3]
            e = g[0] * h[0] + g[1] * h[1] + dy + dz
            return e + jnp.where(row == 0, vv, dn_y(dy)) + jnp.where(lane == 0, vv, dn_z(dz))

        EA[l - 8] = form(ga, ga, a * a)
        EB[l - 8] = form(ga, gb, a * b)
        EC[l - 8] = form(gb, gb, b * b)

    loop(8, 16, forms, 1)
    rho1, zbz, zq = reduce_done(ar1, AR.at[1], 3)
    beta = rho1 / rho0
    pq1 = zbz + 2.0 * beta * zq + beta * beta * pq0
    a1 = rho1 / pq1
    on_z0 = a0 + a1 * beta
    faa, fab, fbb = 0.5 * on_z0 * on_z0, on_z0 * a1, 0.5 * a1 * a1

    def energy(l):
        EN[l] = faa * EA[l] + fab * EB[l] + fbb * EC[l]

    def quarter(x):
        return pl.ds(pl.multiple_of(24 * x, 8), 24)

    mine = quarter(mx)
    pieces = ((0, 3), (3, 6), (6, 8))
    e_energy, e_slope = [], []
    for first, end in pieces:
        loop(first, end, energy, 1)
        part = pl.ds(first, end - first)
        e_energy.append(
            together(
                [
                    (EN.at[part, quarter(lax.rem(mx + o, NLOAD)), :], RS.at[o - 1, part], load(o))
                    for o in range(1, NLOAD)
                ],
                RS.at[:, part],
            )
        )

    def answer(i):
        temp_out[0, i] = on_z0 * Z0[OWN + i] + a1 * X[OWN + i]

    loop(0, 8, answer)

    def total(l):
        e = EN[l, mine, :] + RS[0, l] + RS[1, l] + RS[2, l]
        GB[l + 1, mine, :] = e * DW[l, mine, :]

    for came, (first, end) in zip(e_energy, pieces):
        came.wait_recv()
        loop(first, end, total, end - first)
        copies = []
        for edge, layer, halo, o in ((0, 1, 9, -1), (8, 8, 0, 1)):
            if edge in (first, end):
                copies += [
                    (GB.at[layer, mine, :], GB.at[halo, mine, :], {**block(o), **load(k)}) for k in range(NLOAD)
                ]
        part = GB.at[pl.ds(first + 1, end - first), mine, :]
        size = T0.at[pl.ds(0, 24 * (len(copies) + 3 * (end - first))), :]
        e_slope.append(together(copies + [(part, part, load(o)) for o in range(1, NLOAD)], size))

    def smooth(i):
        s = joined(i + 7) * GB[i] + joined(i + 8) * GB[i + 2]
        slope_out[i] = blur(GB[i + 1], s)

    done_to = 1
    for came, (first, end) in zip(e_slope, pieces):
        came.wait_recv()
        ready = end if end == 8 else end - 1
        loop(done_to, ready, smooth, 1)
        done_to = ready
    smooth(0)
    for c in sent:
        c.wait_send()


def relay(temp, slope, temp_out, slope_out, sem):
    copies = [
        pltpu.make_async_copy(temp, temp_out, sem.at[0]),
        pltpu.make_async_copy(slope, slope_out, sem.at[1]),
    ]
    for c in copies:
        c.start()
    for c in copies:
        c.wait()


def body(design, free_mask, heat_load):
    v = lambda *s: pltpu.VMEM(s, F32)
    brick = v(24, ROWS, 128)
    level1 = v(12, 48, 128)
    level2 = v(WIN * 24, 128)
    level3 = v(160, 128)
    square = pltpu.VMEM((128, 128), BF16)
    scratch = [
        brick, pltpu.VMEM((24, ROWS, 128), jnp.int32), brick,
        brick, brick, brick, brick, brick, brick, brick, brick, brick, brick, brick,
        brick, brick, v(8, ROWS, 128), v(8, ROWS, 128), v(8, ROWS, 128),
        v(ROWS, 128), v(ROWS, 128), v(8, ROWS, 128), v(768, 128), v(768, 128),
        level1, level1, level1, level1, level1, level1, level1, level1, level1,
        v(96, 128), v(2, 144, 128), v(2, 48, 128), v(2, 2, 48, 128), v(2, 48, 128), v(2, 48, 128),
        v(2, 4, 48, 128), v(2, 2, 4, 48, 128), v(WIN, 24, 128), v(24, 128),
        v(2, WIN, 24, 128), v(2, 24, 128),
        level2, level2, level2, level2, level2, level2, level2, v(320, 128),
        level3, level3, level3, level3, level3, v(128, 128),
        v(2, NB, 1, 128), v(8, ROWS, 128), v(3, 8, 24, 128), v(10, ROWS, 128),
        square, square, square, square, square, square, square, square,
        pltpu.SemaphoreType.DMA((3,)), pltpu.SemaphoreType.DMA((22,)), pltpu.SemaphoreType.DMA((22,)),
    ]
    inside = pl.BlockSpec(memory_space=pltpu.VMEM)
    hbm = pl.BlockSpec(memory_space=pltpu.HBM)
    outs = (jax.ShapeDtypeStruct(heat_load.shape, F32), jax.ShapeDtypeStruct(design.shape, F32))
    temp, slope = pl.pallas_call(
        kernel,
        out_shape=(pltpu.VMEM(heat_load.shape, F32), pltpu.VMEM(design.shape, F32)),
        in_specs=[hbm] * 3,
        out_specs=(inside, inside),
        scratch_shapes=scratch,
        compiler_params=pltpu.CompilerParams(
            collective_id=0, has_side_effects=True, vmem_limit_bytes=62 * 2**20
        ),
    )(design, free_mask, heat_load)
    return pl.pallas_call(
        relay,
        out_shape=outs,
        in_specs=[inside] * 2,
        out_specs=(hbm, hbm),
        scratch_shapes=[pltpu.SemaphoreType.DMA((2,))],
        compiler_params=pltpu.CompilerParams(vmem_limit_bytes=4 * 2**20),
    )(temp, slope)


def solution(mesh):
    return jax.shard_map(
        body,
        mesh=mesh,
        in_specs=(P("blocks", None, None), P("blocks", None, None), P("loads", "blocks", None, None)),
        out_specs=(P("loads", "blocks", None, None), P("blocks", None, None)),
        check_vma=False,
    )
```

time: 882 us -> 71.3 us (0.08); the launches traced: 868 us -> 71.2 us
  starting transfers between devices: 224 us -> 0 us
  blocking collectives: 181 us -> 0 us
  local copies, waits for them, and re-layouts: 179 us -> 0 us
  waiting for transfers between devices: 165 us -> 0 us
  other arithmetic: 99.9 us -> 0 us
  Pallas kernels: 0 us -> 70.5 us
  between operations: 19.8 us -> 0.64 us
    ppermute x78 -> x0, starting transfers between devices: 224 us -> none  [the longest x39 136 us: extended(): before = lax.ppermute(last, axis, up)]
    psum x3 -> x0, blocking collectives: 181 us -> none  [inner_total(): return lax.psum(jnp.sum(first_vec * second_vec), 'blocks')]
    reshape x9 -> x0, local copies, waits for them, and re-layouts: 138 us -> none  [the longest x5 91.3 us: restrict_sum(): values.reshape(shape_x // 2, 2, shape_y // 2, 2, shape_z // 2, 2)]
    ppermute x78 -> x0, waiting for transfers between devices: 121 us -> none  [the longest x39 116 us: extended(): after = lax.ppermute(initial, axis, down)]
    pallas_call x0 -> x2, Pallas kernels: none -> 70.5 us  [the longest x1 69.6 us: body(): pl.pallas_call(kernel, out_shape=(pltpu.VMEM(heat_load.shape, F32), pltpu...]
    reduce_sum x15 -> x0, other arithmetic: 50.7 us -> none  [the longest x12 45.5 us: restrict_sum(): values.reshape(shape_x // 2, 2, shape_y // 2, 2, shape_z // 2, 2)]
    psum x1 -> x0, waiting for transfers between devices: 43.7 us -> none  [body(): energy = lax.psum(element_energy, 'loads')]
    broadcast_in_dim x9 -> x0, local copies, waits for them, and re-layouts: 27 us -> none  [the longest x8 26.9 us: prolong(): jnp.broadcast_to(values[:, None, :, None, :, None], (shape_x, 2, shape_y,...]
  transfers between devices with their start and end apart: 79 -> 0, of which waited for: 33 -> 0; matrix products, arithmetic and copies ran while one was open for 12% -> 0% of each run, Pallas kernels for 0% -> 0%
where the time goes in v1:
time: 71.3 us; the launch traced here: 71.2 us
  Pallas kernels  70.5 us (99%)
    pallas_call x1, Pallas kernels, body(): pl.pallas_call(kernel, out_shape=(pltpu.VMEM(heat_load.shape, F32), pltpu...  69.6 us

profile of v1, /device:TPU:1, one launch (start us, length us, event | category | flops | bytes accessed | tf_op | source)
XLA Modules:
  0.0 71.2 jit_solution(10616434871755538002)
XLA Ops:
  0.6 69.6 %shard_map.50 = (f32[1,8,96,128]{3,2,1,0:T(8,128)S(1)}, f32[8,96,128]{2,1,0:T(8,128)S(1)}) custom-call(f32[8,96,128]{2,1,0:T(8,128)} %design.1, s32[8,96,128]{2,1,0:T(8,128)} %mask.1, f32[1,8,96,128]{3,2,1,0:T(8,128)} %heat.1), custom_call_target="tpu_custom_call" | custom-call | tf_op jit(solution)/shard_map/pallas_call | solution.py:735
  70.3 0.9 %shard_map.51 = (f32[1,8,96,128]{3,2,1,0:T(8,128)}, f32[8,96,128]{2,1,0:T(8,128)}) custom-call(f32[1,8,96,128]{3,2,1,0:T(8,128)S(1)} %get-tuple-element.4.temp, f32[8,96,128]{2,1,0:T(8,128)S(1)} %get-tuple-element.5.slope), custom_call_target="tpu_custom_call" | custom-call | tf_op jit(solution)/shard_map/pallas_call | solution.py:745

commit v2 on v1

--- a/solution.py
+++ b/solution.py
@@ -49,9 +49,8 @@
     hi = x.astype(BF16)
     rest = x - hi.astype(F32)
     mid = rest.astype(BF16)
-    low = (rest - mid.astype(F32)).astype(BF16)
     d = lambda a: jnp.dot(a, m, preferred_element_type=F32)
-    return d(hi) + d(mid) + d(low)
+    return d(hi) + d(mid)
 
 
 def stencil(x, xm, xp, cxm, cx, cy, cz):

time: 71.3 us -> 70.8 us (level)
  no operation moved by 1% of the time
where the time goes in v2:
time: 70.8 us; the launch traced here: 70.7 us
  Pallas kernels  70.1 us (99%)
    pallas_call x1, Pallas kernels, body(): pl.pallas_call(kernel, out_shape=(pltpu.VMEM(heat_load.shape, F32), pltpu...  69.2 us

profile of v2, /device:TPU:1, one launch (start us, length us, event | category | flops | bytes accessed | tf_op | source)
XLA Modules:
  0.0 70.7 jit_solution(2872479906589799653)
XLA Ops:
  0.6 69.2 %shard_map.50 = (f32[1,8,96,128]{3,2,1,0:T(8,128)S(1)}, f32[8,96,128]{2,1,0:T(8,128)S(1)}) custom-call(f32[8,96,128]{2,1,0:T(8,128)} %design.1, s32[8,96,128]{2,1,0:T(8,128)} %mask.1, f32[1,8,96,128]{3,2,1,0:T(8,128)} %heat.1), custom_call_target="tpu_custom_call" | custom-call | tf_op jit(solution)/shard_map/pallas_call | solution.py:734
  69.8 0.9 %shard_map.51 = (f32[1,8,96,128]{3,2,1,0:T(8,128)}, f32[8,96,128]{2,1,0:T(8,128)}) custom-call(f32[1,8,96,128]{3,2,1,0:T(8,128)S(1)} %get-tuple-element.4.temp, f32[8,96,128]{2,1,0:T(8,128)S(1)} %get-tuple-element.5.slope), custom_call_target="tpu_custom_call" | custom-call | tf_op jit(solution)/shard_map/pallas_call | solution.py:744

commit v3 on v2

--- a/solution.py
+++ b/solution.py
@@ -550,13 +550,6 @@
     loop(5, 9, image)
     loop(15, 19, image)
 
-    def inner0(i, c):
-        l = OWN + i
-        z = Z0[l]
-        return c[0] + fold(B0[l] * z), c[1] + fold(z * Q0[l])
-
-    nil = jnp.zeros((8, 128), F32)
-    ar0 = reduce_start(lax.fori_loop(0, 8, inner0, (nil, nil)), AR.at[0])
     pre = sweep0(X, Y, Q0)
     mismatch0 = residual0(Y, Q0, 4)
     loop(6, 18, pre)
@@ -573,18 +566,27 @@
     g_two = gather(MG.at[1], R.at[1])
     e_m2 = together([(MP.at[1], MR.at[1, 0], block(1)), (MP.at[1], MR.at[1, 1], block(-1))], MR.at[1])
 
+    def inner0(i, c):
+        l = OWN + i
+        z = Z0[l]
+        return c[0] + fold(B0[l] * z), c[1] + fold(z * Q0[l])
+
+    nil = jnp.zeros((8, 128), F32)
+    ar0 = reduce_start(lax.fori_loop(0, 8, inner0, (nil, nil)), AR.at[0])
+
     def masked(l):
         VA[l] = free(l) * Z0[l]
 
     loop(7, 17, masked)
-    rho0, pq0 = reduce_done(ar0, AR.at[0], 2)
-    a0 = rho0 / pq0
     g_two.wait_recv()
     coarse(R.at[1])
     e_m2.wait_recv()
     level1_up(MR.at[1], 0)
     spread0(2, 8)
     loop(6, 18, sweep0(X, Y, Q0))
+
+    rho0, pq0 = reduce_done(ar0, AR.at[0], 2)
+    a0 = rho0 / pq0
 
     def last_sweep(l):
         w = Y[l] * THIRD + G[l] * (Q0[l] + apply0(Y, l))

time: 70.8 us -> 70.3 us (level)
  no operation moved by 1% of the time
where the time goes in v3:
time: 70.3 us; the launch traced here: 70.2 us
  Pallas kernels  69.5 us (99%)
    pallas_call x1, Pallas kernels, body(): pl.pallas_call(kernel, out_shape=(pltpu.VMEM(heat_load.shape, F32), pltpu...  68.6 us

profile of v3, /device:TPU:1, one launch (start us, length us, event | category | flops | bytes accessed | tf_op | source)
XLA Modules:
  0.0 70.2 jit_solution(456520990868175162)
XLA Ops:
  0.6 68.6 %shard_map.50 = (f32[1,8,96,128]{3,2,1,0:T(8,128)S(1)}, f32[8,96,128]{2,1,0:T(8,128)S(1)}) custom-call(f32[8,96,128]{2,1,0:T(8,128)} %design.1, s32[8,96,128]{2,1,0:T(8,128)} %mask.1, f32[1,8,96,128]{3,2,1,0:T(8,128)} %heat.1), custom_call_target="tpu_custom_call" | custom-call | tf_op jit(solution)/shard_map/pallas_call | solution.py:736
  69.3 0.9 %shard_map.51 = (f32[1,8,96,128]{3,2,1,0:T(8,128)}, f32[8,96,128]{2,1,0:T(8,128)}) custom-call(f32[1,8,96,128]{3,2,1,0:T(8,128)S(1)} %get-tuple-element.4.temp, f32[8,96,128]{2,1,0:T(8,128)S(1)} %get-tuple-element.5.slope), custom_call_target="tpu_custom_call" | custom-call | tf_op jit(solution)/shard_map/pallas_call | solution.py:746

commit v4 on v3

--- a/solution.py
+++ b/solution.py
@@ -179,7 +179,7 @@
         lane = lanes((1, 128))
         row = jnp.zeros((1, 128), F32)
         for i, v in enumerate(values):
-            row = jnp.where(lane == i, jnp.sum(v), row)
+            row = jnp.where(lane == i, jnp.sum(v, axis=(0, 1), keepdims=True), row)
         buf[me] = row
 
         def send(i, c):
@@ -349,14 +349,12 @@
 
         loop(1, 11, one_layer)
 
-    def level1_down(msg, packed):
+    def level1_down(msg):
         def start(l):
             X1[l] = G1[l] * B1[l]
 
         loop(2, 10, start, 4)
         loop(3, 9, sweep1(X1, Y1))
-        for l in range(4):
-            packed[l] = Y1[4 + l] + pltpu.roll(B1[4 + l], 64, 1)
 
         def mismatch(i):
             l = 4 + i
@@ -500,8 +498,10 @@
     for side, base in ((0, 2), (1, 8)):
         B1[base] = BR[side]
         B1[base + 1] = pltpu.roll(BR[side], 64, 1)
-    level1_down(MG.at[0], MP.at[0])
+    level1_down(MG.at[0])
     g_one = gather(MG.at[0], R.at[0])
+    for l in range(4):
+        MP[0, l] = Y1[4 + l] + pltpu.roll(B1[4 + l], 64, 1)
     e_m1 = together([(MP.at[0], MR.at[0, 0], block(1)), (MP.at[0], MR.at[0, 1], block(-1))], MR.at[0])
 
     e_rest = together(rim(D, 0, 3) + rim(MK, 1, 4), layers(12))
@@ -562,8 +562,10 @@
     loop(0, 2, mismatch0, 1)
     loop(6, 8, mismatch0, 1)
     B1[pl.ds(2, 8)] = pair_z1(8, 0.5)
-    level1_down(MG.at[1], MP.at[1])
+    level1_down(MG.at[1])
     g_two = gather(MG.at[1], R.at[1])
+    for l in range(4):
+        MP[1, l] = Y1[4 + l] + pltpu.roll(B1[4 + l], 64, 1)
     e_m2 = together([(MP.at[1], MR.at[1, 0], block(1)), (MP.at[1], MR.at[1, 1], block(-1))], MR.at[1])
 
     def inner0(i, c):

time: 70.3 us -> 70.3 us (level)
  no operation moved by 1% of the time
where the time goes in v4:
time: 70.3 us; the launch traced here: 70.1 us
  Pallas kernels  69.5 us (99%)
    pallas_call x1, Pallas kernels, body(): pl.pallas_call(kernel, out_shape=(pltpu.VMEM(heat_load.shape, F32), pltpu...  68.6 us

profile of v4, /device:TPU:1, one launch (start us, length us, event | category | flops | bytes accessed | tf_op | source)
XLA Modules:
  0.0 70.1 jit_solution(1487575454631260202)
XLA Ops:
  0.6 68.6 %shard_map.50 = (f32[1,8,96,128]{3,2,1,0:T(8,128)S(1)}, f32[8,96,128]{2,1,0:T(8,128)S(1)}) custom-call(f32[8,96,128]{2,1,0:T(8,128)} %design.1, s32[8,96,128]{2,1,0:T(8,128)} %mask.1, f32[1,8,96,128]{3,2,1,0:T(8,128)} %heat.1), custom_call_target="tpu_custom_call" | custom-call | tf_op jit(solution)/shard_map/pallas_call | solution.py:738
  69.3 0.9 %shard_map.51 = (f32[1,8,96,128]{3,2,1,0:T(8,128)}, f32[8,96,128]{2,1,0:T(8,128)}) custom-call(f32[1,8,96,128]{3,2,1,0:T(8,128)S(1)} %get-tuple-element.4.temp, f32[8,96,128]{2,1,0:T(8,128)S(1)} %get-tuple-element.5.slope), custom_call_target="tpu_custom_call" | custom-call | tf_op jit(solution)/shard_map/pallas_call | solution.py:748
